TPU v7x, 32 devices: a whole 2x2x4 slice. The times are simulated.
32 devices in a mesh: section: 2 (over x), dp: 4 (over z), tensor: 4 (over y, core).
Axes of the slice: x: 2, y: 2, z: 4, core: 2. Of those that a mesh axis runs over, the one named last changes fastest.
Arguments:
- tokens: bfloat16 [2, 1024, 768], P(None, ('dp', 'tensor')), may hold values from -6 to 6
- cotangent: bfloat16 [2, 1024, 768], P(None, ('dp', 'tensor')), may hold values from -6 to 6
- w_qkv: bfloat16 [2, 3, 768, 768], P('section', None, 'dp', 'tensor'), may hold values from -0.21875 to 0.21875
- w_out: bfloat16 [2, 768, 768], P('section', 'tensor', 'dp'), may hold values from -1.75 to 1.75
- w_gate_up: bfloat16 [2, 2, 768, 3072], P('section', None, 'dp', 'tensor'), may hold values from -0.21875 to 0.21875
- w_down: bfloat16 [2, 3072, 768], P('section', 'tensor', 'dp'), may hold values from -0.109375 to 0.109375
- rel_table: bfloat16 [2, 32, 12], P('section', 'dp', 'tensor'), may hold values from -4 to 4
- gains: bfloat16 [2, 3, 768], P('section', None, ('dp', 'tensor')), may hold values from 0.25 to 1.75
- router: bfloat16 [2, 768, 8], P('section', ('dp', 'tensor')), may hold values from -0.21875 to 0.21875
- w_in: bfloat16 [2, 8, 768, 3072], P('section', 'dp', None, 'tensor'), may hold values from -0.21875 to 0.21875
- w_expert_out: bfloat16 [2, 8, 3072, 768], P('section', 'dp', 'tensor'), may hold values from -0.109375 to 0.109375
- routes: int32 [2, 2, 1024, 2], P('section', None, 'dp'), may hold values from 0 to 7, all different within a row; in each aligned block of 256 rows (0 to 255, 256 to 511, ..., all dimensions but the last counted through in order) at most 80 rows name the same one
Outputs:
- block_out: bfloat16 [2, 2, 1024, 768], P('section', None, ('dp', 'tensor'))
- input_grads: bfloat16 [2, 2, 1024, 768], P('section', None, ('dp', 'tensor'))
- grad_w_qkv: float32 [2, 3, 768, 768], P('section', None, 'dp', 'tensor')
- grad_w_out: float32 [2, 768, 768], P('section', 'tensor', 'dp')
- grad_w_gate_up: float32 [2, 2, 768, 3072], P('section', None, 'dp', 'tensor')
- grad_w_down: float32 [2, 3072, 768], P('section', 'tensor', 'dp')
- grad_rel_table: float32 [2, 32, 12], P('section', 'dp', 'tensor')
- grad_gains: float32 [2, 3, 768], P('section', None, ('dp', 'tensor'))
- grad_router: float32 [2, 768, 8], P('section', ('dp', 'tensor'))
- grad_w_in: float32 [2, 8, 768, 3072], P('section', 'dp', None, 'tensor')
- grad_w_expert_out: float32 [2, 8, 3072, 768], P('section', 'dp', 'tensor')
Inputs may be any that keep to these rules, and one draw needn't show every extreme that they name: `routes`: each row names 2 different experts; within each aligned block of 256 rows (one micro-batch's tokens of one dp index) no expert is named more than 80 times.
All inputs are finite; a program needn't handle non-finite values.
Results may differ from a plain program's by a relative error of at most 0.033.
Values may be sent and summed in bfloat16 or wider, within the bound.
A program may use at most 256 MiB of HBM per device.

v0:
```python
import jax
import jax.numpy as jnp
import numpy as np
from jax import lax
from jax.sharding import PartitionSpec as P

HD = 64
NB = 32
MAXDIST = 128


highest_precision = lax.Precision.HIGHEST
norm_eps = 1e-06
masked_score = -1000000000.0


def from_behind(value, axis, steps):
    count = lax.axis_size(axis)
    first, last = (max(0, -steps), min(count, count - steps))
    return lax.ppermute(value, axis, [(source, source + steps) for source in range(first, last)])


def bucket_edges():
    exact_span = NB // 2
    distance = np.arange(1, 4 * MAXDIST + 1) * 1.0
    log_ratio = np.log(np.maximum(distance, exact_span) / exact_span) / np.log(MAXDIST / exact_span)
    far_bucket = np.minimum(exact_span + np.floor(log_ratio * (NB - exact_span)), NB - 1)
    bucket = np.where(distance < exact_span, distance, far_bucket)
    return [int(distance[np.argmax(bucket >= bucket_no)]) for bucket_no in range(1, NB)]


def relative_bucket(distance):
    bucket = jnp.zeros(distance.shape, jnp.int32)
    for edge_at in bucket_edges():
        bucket = bucket + (distance >= edge_at).astype(jnp.int32)
    return bucket


def norm_rows(hidden_in, gain_row):
    return (
        hidden_in
        * lax.rsqrt(jnp.mean(hidden_in * hidden_in, axis=-1, keepdims=True) + norm_eps)
        * gain_row
    )


def gelu_tanh(inputs):
    return jax.nn.gelu(inputs, approximate=True)


def gated(gate_part, up_part):
    return gelu_tanh(gate_part) * up_part


def gate_weights(logits, route_rows):
    chosen = route_rows[:, :, None] == jnp.arange(logits.shape[1], dtype=jnp.int32)[None, None, :]
    picked = jnp.sum(jnp.where(chosen, logits[:, None, :], 0.0), axis=2)
    row_max = jnp.max(picked, axis=1, keepdims=True)
    raised = jnp.exp(picked - row_max)
    return (raised / jnp.sum(raised, axis=1, keepdims=True), chosen)


def send_rows(part):
    return lax.all_to_all(part, "dp", split_axis=0, concat_axis=0, tiled=True)


def send_results(part):
    return lax.all_to_all(
        part.astype(jnp.bfloat16), "dp", split_axis=0, concat_axis=0, tiled=True
    ).astype(part.dtype)


def on_device(
    tokens,
    cotangent,
    w_qkv,
    w_out,
    w_gate_up,
    w_down,
    rel_table,
    gains,
    router,
    w_in,
    w_expert_out,
    routes,
):
    dp_count = lax.axis_size("dp")
    tensor_count = lax.axis_size("tensor")
    dp_place = lax.axis_index("dp")
    is_first = lax.axis_index("section") == 0
    micro_count = tokens.shape[0]
    local_rows = tokens.shape[1]
    model = tokens.shape[2]
    tok_dp = local_rows * tensor_count
    seq_span = min(4, dp_count)
    length = tok_dp * seq_span
    expert_count = router.shape[2]
    top_count = routes.shape[3]
    capacity = (5 * tok_dp * top_count + 4 * expert_count - 1) // (4 * expert_count)
    gathered = (
        lax.all_gather(w_qkv, "dp", axis=2, tiled=True),
        lax.all_gather(w_out, "dp", axis=2, tiled=True),
        lax.all_gather(w_gate_up, "dp", axis=2, tiled=True),
        lax.all_gather(w_down, "dp", axis=2, tiled=True),
        lax.all_gather(rel_table, "dp", axis=1, tiled=True),
    )
    shared = (
        lax.all_gather(gains, ("dp", "tensor"), axis=2, tiled=True),
        lax.all_gather(router, ("dp", "tensor"), axis=1, tiled=True),
    )
    qkv_weight = gathered[0][0]
    out_weight = gathered[1][0]
    gate_up_weight = gathered[2][0]
    down_weight = gathered[3][0]
    table_low = gathered[4][0]
    position_table = table_low.astype(jnp.float32)
    gain_all = shared[0][0].astype(jnp.float32)
    router_all = shared[1][0]
    router_wide = router_all.astype(jnp.float32)
    inner_weight = w_in[0]
    outer_weight = w_expert_out[0]
    head_count = position_table.shape[1]
    head_width = head_count * HD
    seq_start = dp_place // seq_span * length
    query_start = dp_place * tok_dp
    scale = HD ** (-0.5)

    def rows_in(part):
        return lax.all_gather(part, "tensor", axis=0, tiled=True)

    def rows_out(part):
        return lax.psum_scatter(part, "tensor", scatter_dimension=0, tiled=True)

    def score_rows(queries, key_rows, key_start):
        key_count = key_rows.shape[0]
        window = min(key_count, tok_dp + MAXDIST)
        window_start = jnp.clip(query_start - key_start - (window - tok_dp), 0, key_count - window)
        raw_scores = (
            jnp.einsum("qhd,khd->hqk", queries, key_rows, preferred_element_type=jnp.float32)
            * scale
        )
        query_pos = query_start + jnp.arange(tok_dp, dtype=jnp.int32)
        near_pos = key_start + window_start + jnp.arange(window, dtype=jnp.int32)
        near_bucket = relative_bucket(query_pos[:, None] - near_pos[None, :])
        one_hot_matrix = (
            near_bucket[None, :, :] == jnp.arange(NB, dtype=jnp.int32)[:, None, None]
        ).astype(jnp.bfloat16)
        nearby_bias = jnp.einsum(
            "vod,vl->lod", one_hot_matrix, table_low, preferred_element_type=jnp.float32
        )
        near_scores = lax.dynamic_slice_in_dim(raw_scores, window_start, window, 2) + nearby_bias
        scores = raw_scores + position_table[NB - 1][:, None, None]
        scores = lax.dynamic_update_slice_in_dim(scores, near_scores, window_start, 2)
        key_pos = key_start + jnp.arange(key_count, dtype=jnp.int32)
        allowed = (key_pos[None, :] <= query_pos[:, None]) & (key_pos[None, :] >= seq_start)
        return (jnp.where(allowed[None], scores, masked_score), one_hot_matrix, window_start)

    def attend_back(queries, pair_rows, key_start, log_total, grad_attended):
        key_count = pair_rows.shape[0]
        pairs = pair_rows.reshape(key_count, 2, head_count, HD)
        scores, one_hot_matrix, window_start = score_rows(queries, pairs[:, 0], key_start)
        soft = jnp.exp(scores - log_total)
        grad_soft = jnp.einsum(
            "qhd,khd->hqk", grad_attended, pairs[:, 1], preferred_element_type=jnp.float32
        )
        inner_sum = jnp.sum(soft * grad_soft, axis=2, keepdims=True)
        grad_scores = (soft * (grad_soft - inner_sum)).astype(jnp.bfloat16)
        window = one_hot_matrix.shape[2]
        nearby_gradient = lax.dynamic_slice_in_dim(grad_scores, window_start, window, 2)
        table_gradient = jnp.einsum(
            "ptm,stm->ps", one_hot_matrix, nearby_gradient, preferred_element_type=jnp.float32
        )
        far_sum = jnp.sum(grad_scores, axis=(1, 2), dtype=jnp.float32) - jnp.sum(
            nearby_gradient, axis=(1, 2), dtype=jnp.float32
        )
        table_gradient = table_gradient.at[NB - 1].add(far_sum)
        grad_queries = (
            jnp.einsum("hqk,khd->qhd", grad_scores, pairs[:, 0], preferred_element_type=jnp.float32)
            * scale
        )
        grad_keys = (
            jnp.einsum("hqk,qhd->khd", grad_scores, queries, preferred_element_type=jnp.float32)
            * scale
        )
        grad_values = jnp.einsum(
            "hqk,qhd->khd",
            soft.astype(jnp.bfloat16),
            grad_attended,
            preferred_element_type=jnp.float32,
        )
        grad_pairs = jnp.stack([grad_keys, grad_values], axis=1).reshape(key_count, 2 * head_width)
        return (grad_queries.reshape(tok_dp, head_width), grad_pairs, table_gradient)

    outputs = []
    kept_ticks = []
    arrived_rows = jnp.zeros_like(tokens[0])
    for tick_no in range(micro_count + 1):
        section_input = jnp.where(is_first, tokens[min(tick_no, micro_count - 1)], arrived_rows)
        route_rows = jnp.where(
            is_first, routes[0, min(tick_no, micro_count - 1)], routes[0, max(tick_no - 1, 0)]
        )
        forward_residual = section_input.astype(jnp.float32)
        forward_rows_attn = rows_in(norm_rows(forward_residual, gain_all[0]).astype(jnp.bfloat16))
        projected = jnp.einsum(
            "td,cdf->ctf", forward_rows_attn, qkv_weight, preferred_element_type=jnp.float32
        ).astype(jnp.bfloat16)
        forward_queries = projected[0].reshape(tok_dp, head_count, HD)
        everything = lax.all_gather(
            jnp.concatenate([projected[1], projected[2]], axis=1), "dp", axis=0, tiled=True
        )
        fetched = lax.dynamic_slice_in_dim(everything, seq_start, length, 0)
        attend_pairs = fetched.reshape(fetched.shape[0], 2, head_count, HD)
        attend_scores, attend_one_hot_matrix, attend_window_start = score_rows(
            forward_queries, attend_pairs[:, 0], seq_start
        )
        row_max = jnp.max(attend_scores, axis=2, keepdims=True)
        attend_log_total = row_max + jnp.log(
            jnp.sum(jnp.exp(attend_scores - row_max), axis=2, keepdims=True)
        )
        attend_soft = jnp.exp(attend_scores - attend_log_total).astype(jnp.bfloat16)
        attend_attended = jnp.einsum(
            "hqk,khd->qhd", attend_soft, attend_pairs[:, 1], preferred_element_type=jnp.float32
        )
        forward_attended = attend_attended.reshape(tok_dp, head_width).astype(jnp.bfloat16)
        forward_residual1 = forward_residual + rows_out(
            jnp.dot(forward_attended, out_weight, preferred_element_type=jnp.float32)
        )
        forward_rows_mlp = rows_in(norm_rows(forward_residual1, gain_all[1]).astype(jnp.bfloat16))
        forward_gate_up = jnp.einsum(
            "td,cdf->ctf", forward_rows_mlp, gate_up_weight, preferred_element_type=jnp.float32
        )
        forward_hidden = gated(forward_gate_up[0], forward_gate_up[1]).astype(jnp.bfloat16)
        forward_residual2 = forward_residual1 + rows_out(
            jnp.dot(forward_hidden, down_weight, preferred_element_type=jnp.float32)
        )
        forward_rows_moe = rows_in(norm_rows(forward_residual2, gain_all[2]).astype(jnp.bfloat16))
        logits = jnp.dot(forward_rows_moe, router_all, preferred_element_type=jnp.float32)
        forward_gate_probs, forward_chosen = gate_weights(logits, route_rows)
        flat = route_rows.reshape(-1)
        expert_one_hot_matrix = (
            flat[:, None] == jnp.arange(expert_count, dtype=jnp.int32)[None, :]
        ).astype(jnp.int32)
        before = jnp.cumsum(expert_one_hot_matrix, axis=0) - expert_one_hot_matrix
        forward_slot_ids = flat * capacity + jnp.sum(before * expert_one_hot_matrix, axis=1)
        forward_outgoing = (
            jnp.zeros((expert_count * capacity, model), jnp.bfloat16)
            .at[forward_slot_ids]
            .set(jnp.repeat(forward_rows_moe, top_count, axis=0))
        )
        forward_arrived = send_rows(forward_outgoing.reshape(dp_count, -1, model))
        forward_arrived = forward_arrived.reshape(dp_count, -1, capacity, model)
        forward_before_act = jnp.einsum(
            "secd,edf->secf", forward_arrived, inner_weight, preferred_element_type=jnp.float32
        )
        forward_active = gelu_tanh(forward_before_act).astype(jnp.bfloat16)
        results = jnp.einsum(
            "secf,efd->secd", forward_active, outer_weight, preferred_element_type=jnp.float32
        )
        returned = send_results(results.reshape(dp_count, -1, model))
        forward_picked_rows = returned.reshape(expert_count * capacity, model)[
            forward_slot_ids
        ].reshape(tok_dp, top_count, model)
        residual3 = forward_residual2 + rows_out(
            jnp.sum(forward_gate_probs[:, :, None] * forward_picked_rows, axis=1)
        )
        forward_kept = (
            forward_residual,
            forward_rows_attn,
            forward_queries,
            fetched,
            seq_start,
            attend_log_total,
            forward_attended,
            forward_residual1,
            forward_rows_mlp,
            forward_gate_up,
            forward_hidden,
            forward_residual2,
            forward_rows_moe,
            forward_gate_probs,
            forward_chosen,
            forward_slot_ids,
            forward_picked_rows,
            forward_arrived,
            forward_before_act,
            forward_active,
        )
        result = residual3.astype(jnp.bfloat16)
        kept = forward_kept
        outputs.append(result)
        kept_ticks.append(kept)
        if tick_no < micro_count:
            arrived_rows = from_behind(result, "section", 1)
    grad_sums = (
        jnp.zeros(qkv_weight.shape, jnp.float32),
        jnp.zeros(out_weight.shape, jnp.float32),
        jnp.zeros(gate_up_weight.shape, jnp.float32),
        jnp.zeros(down_weight.shape, jnp.float32),
        jnp.zeros(position_table.shape, jnp.float32),
        jnp.zeros(gain_all.shape, jnp.float32),
        jnp.zeros(router_all.shape, jnp.float32),
        jnp.zeros(inner_weight.shape, jnp.float32),
        jnp.zeros(outer_weight.shape, jnp.float32),
    )
    returned_grad = jnp.zeros_like(tokens[0])
    input_list = []
    for tick_no in range(micro_count + 1):
        if tick_no < micro_count:
            outer_cot = cotangent[tick_no]
        else:
            outer_cot = jnp.zeros_like(cotangent[0])
        upstream = jnp.where(is_first, returned_grad, outer_cot)
        kept = jax.tree.map(
            lambda early, late: jnp.where(is_first, early, late),
            kept_ticks[max(tick_no - 1, 0)],
            kept_ticks[min(tick_no + 1, micro_count)],
        )
        (
            residual,
            rows_attn,
            backward_queries,
            backward_pair_rows,
            backward_key_start,
            backward_log_total,
            attended,
            residual1,
            rows_mlp,
            gate_up,
            hidden,
            residual2,
            rows_moe,
            gate_probs,
            chosen,
            slot_ids,
            picked_rows,
            arrived,
            before_act,
            active,
        ) = kept
        grad3 = upstream.astype(jnp.float32)
        rows_grad3 = rows_in(upstream)
        wide_grad3 = rows_grad3.astype(jnp.float32)
        to_experts = (gate_probs[:, :, None] * wide_grad3[:, None, :]).astype(jnp.bfloat16)
        outgoing = (
            jnp.zeros((expert_count * capacity, model), jnp.bfloat16)
            .at[slot_ids]
            .set(to_experts.reshape(-1, model))
        )
        grad_results = send_rows(outgoing.reshape(dp_count, -1, model))
        grad_results = grad_results.reshape(dp_count, -1, capacity, model)
        grad_gate = jnp.sum(wide_grad3[:, None, :] * picked_rows, axis=2)
        grad_active = jnp.einsum(
            "secd,efd->secf", grad_results, outer_weight, preferred_element_type=jnp.float32
        )
        outer_grad = jnp.einsum(
            "secf,secd->efd", active, grad_results, preferred_element_type=jnp.float32
        )
        gelu_back = jax.vjp(gelu_tanh, before_act)[1]
        grad_before = gelu_back(grad_active)[0].astype(jnp.bfloat16)
        inner_grad = jnp.einsum(
            "secd,secf->edf", arrived, grad_before, preferred_element_type=jnp.float32
        )
        grad_arrived = jnp.einsum(
            "secf,edf->secd", grad_before, inner_weight, preferred_element_type=jnp.float32
        )
        grad_back = send_results(grad_arrived.reshape(dp_count, -1, model))
        grad_copies = grad_back.reshape(expert_count * capacity, model)[slot_ids].reshape(
            tok_dp, top_count, model
        )
        grad_picked = gate_probs * (
            grad_gate - jnp.sum(gate_probs * grad_gate, axis=1, keepdims=True)
        )
        grad_logits = jnp.sum(jnp.where(chosen, grad_picked[:, :, None], 0.0), axis=1)
        router_grad = jnp.dot(
            rows_moe.astype(jnp.float32).T, grad_logits, precision=highest_precision
        )
        grad_moe_rows = jnp.sum(grad_copies, axis=1) + jnp.dot(
            grad_logits, router_wide.T, precision=highest_precision
        )
        norm_back = jax.vjp(norm_rows, residual2, gain_all[2])[1]
        grad_residual2, gain_grad2 = norm_back(rows_out(grad_moe_rows))
        grad2 = grad3 + grad_residual2
        rows_grad2 = rows_in(grad2.astype(jnp.bfloat16))
        grad_hidden = jnp.einsum(
            "td,fd->tf", rows_grad2, down_weight, preferred_element_type=jnp.float32
        )
        down_grad = jnp.einsum("tf,td->fd", hidden, rows_grad2, preferred_element_type=jnp.float32)
        gated_back = jax.vjp(gated, gate_up[0], gate_up[1])[1]
        grad_gate_up = jnp.stack(gated_back(grad_hidden)).astype(jnp.bfloat16)
        gate_up_grad = jnp.einsum(
            "td,ctf->cdf", rows_mlp, grad_gate_up, preferred_element_type=jnp.float32
        )
        grad_mid = rows_out(
            jnp.einsum(
                "ctf,cdf->td", grad_gate_up, gate_up_weight, preferred_element_type=jnp.float32
            )
        )
        norm_back = jax.vjp(norm_rows, residual1, gain_all[1])[1]
        grad_residual1, gain_grad1 = norm_back(grad_mid)
        grad1 = grad2 + grad_residual1
        rows_grad1 = rows_in(grad1.astype(jnp.bfloat16))
        backward_grad_attended = jnp.einsum(
            "td,fd->tf", rows_grad1, out_weight, preferred_element_type=jnp.float32
        ).astype(jnp.bfloat16)
        output_gradient = jnp.einsum(
            "tf,td->fd", attended, rows_grad1, preferred_element_type=jnp.float32
        )
        backward_grad_queries, backward_grad_pairs, backward_table_gradient = attend_back(
            backward_queries,
            backward_pair_rows,
            backward_key_start,
            backward_log_total,
            backward_grad_attended.reshape(tok_dp, head_count, HD),
        )
        spread_rows = jnp.zeros((dp_count * tok_dp, backward_grad_pairs.shape[1]), jnp.float32)
        spread_rows = lax.dynamic_update_slice_in_dim(
            spread_rows, backward_grad_pairs, seq_start, 0
        )
        own_rows = lax.psum_scatter(
            spread_rows.astype(jnp.bfloat16), "dp", scatter_dimension=0, tiled=True
        ).astype(jnp.float32)
        grad_project = jnp.stack(
            [backward_grad_queries, own_rows[:, :head_width], own_rows[:, head_width:]]
        ).astype(jnp.bfloat16)
        qkv_grad = jnp.einsum(
            "td,ctf->cdf", rows_attn, grad_project, preferred_element_type=jnp.float32
        )
        grad_norm0 = rows_out(
            jnp.einsum("ctf,cdf->td", grad_project, qkv_weight, preferred_element_type=jnp.float32)
        )
        norm_back = jax.vjp(norm_rows, residual, gain_all[0])[1]
        grad_residual0, gain_grad0 = norm_back(grad_norm0)
        grad0 = grad1 + grad_residual0
        gain_grad = jnp.stack([gain_grad0, gain_grad1, gain_grad2])
        step_grads = (
            qkv_grad,
            output_gradient,
            gate_up_grad,
            down_grad,
            backward_table_gradient,
            gain_grad,
            router_grad,
            inner_grad,
            outer_grad,
        )
        grad_input, step_grads = (grad0.astype(jnp.bfloat16), step_grads)
        grad_sums = jax.tree.map(jnp.add, grad_sums, step_grads)
        input_list.append(grad_input)
        if tick_no < micro_count:
            returned_grad = from_behind(grad_input, "section", -1)
    block_out = jnp.stack(
        [
            jnp.where(is_first, outputs[micro_no], outputs[micro_no + 1])
            for micro_no in range(micro_count)
        ]
    )[None]
    input_grads = jnp.stack(
        [
            jnp.where(is_first, input_list[micro_no + 1], input_list[micro_no])
            for micro_no in range(micro_count)
        ]
    )[None]
    dense_grads = (
        lax.psum_scatter(
            grad_sums[0][None].astype(jnp.bfloat16), "dp", scatter_dimension=2, tiled=True
        ).astype(jnp.float32),
        lax.psum_scatter(
            grad_sums[1][None].astype(jnp.bfloat16), "dp", scatter_dimension=2, tiled=True
        ).astype(jnp.float32),
        lax.psum_scatter(
            grad_sums[2][None].astype(jnp.bfloat16), "dp", scatter_dimension=2, tiled=True
        ).astype(jnp.float32),
        lax.psum_scatter(
            grad_sums[3][None].astype(jnp.bfloat16), "dp", scatter_dimension=2, tiled=True
        ).astype(jnp.float32),
        lax.psum_scatter(
            grad_sums[4][None].astype(jnp.bfloat16), "dp", scatter_dimension=1, tiled=True
        ).astype(jnp.float32),
    )
    small_grads = (
        lax.psum_scatter(grad_sums[5][None], ("dp", "tensor"), scatter_dimension=2, tiled=True),
        lax.psum_scatter(grad_sums[6][None], ("dp", "tensor"), scatter_dimension=1, tiled=True),
    )
    return (
        block_out,
        input_grads,
        dense_grads[0],
        dense_grads[1],
        dense_grads[2],
        dense_grads[3],
        dense_grads[4],
        small_grads[0],
        small_grads[1],
        grad_sums[7][None],
        grad_sums[8][None],
    )


def solution(mesh):
    placed = (
        P(None, ("dp", "tensor"), None),
        P(None, ("dp", "tensor"), None),
        P("section", None, "dp", "tensor"),
        P("section", "tensor", "dp"),
        P("section", None, "dp", "tensor"),
        P("section", "tensor", "dp"),
        P("section", "dp", "tensor"),
        P("section", None, ("dp", "tensor")),
        P("section", ("dp", "tensor"), None),
        P("section", "dp", None, "tensor"),
        P("section", "dp", "tensor", None),
        P("section", None, "dp", None),
    )
    return jax.shard_map(
        on_device,
        mesh=mesh,
        in_specs=placed,
        out_specs=(
            P("section", None, ("dp", "tensor"), None),
            P("section", None, ("dp", "tensor"), None),
            P("section", None, "dp", "tensor"),
            P("section", "tensor", "dp"),
            P("section", None, "dp", "tensor"),
            P("section", "tensor", "dp"),
            P("section", "dp", "tensor"),
            P("section", None, ("dp", "tensor")),
            P("section", ("dp", "tensor"), None),
            P("section", "dp", None, "tensor"),
            P("section", "dp", "tensor", None),
        ),
        check_vma=False,
    )
```

profile of v0, /device:TPU:0, one launch (start us, length us, event | category | flops | bytes accessed | tf_op | source)
XLA Modules:
  0.0 1779.5 jit_solution(10360349430326636469)
XLA Ops:
  25.3 22.5 %all_gather.84 = bf16[1,3,768]{1,0,2:T(2,128)(2,1)S(1)} all-gather(bf16[1,3,48]{1,0,2:T(2,128)(2,1)S(1)} %copy.210), channel_id=1, replica_groups=mesh['section'=2,'dp'=4,'tensor'=4] {'dp','tensor'}, dimensions={2}, use_global_device_ids=true | all-gather | bytes 4896 | tf_op jit(solution)/shard_map/all_gather | solution.py:108
  63.4 30.2 %all_gather.86 = bf16[1,3,768,192]{3,1,0,2:T(4,128)(2,1)} all-gather(bf16[1,3,192,192]{3,1,0,2:T(4,128)(2,1)S(1)} %copy.211), channel_id=1, replica_groups=mesh['section'=2,'dp'=4,'tensor'=4] {'dp'}, dimensions={2}, use_global_device_ids=true | all-gather | bytes 1105920 | tf_op jit(solution)/shard_map/all_gather | solution.py:101
  218.0 26.7 %all-gather.6.cloned.1.call-done = bf16[1,768,768]{1,2,0:T(8,128)(2,1)} async-done(((bf16[1,768,192]{1,2,0:T(8,128)(2,1)}), bf16[1,768,768]{1,2,0:T(8,128)(2,1)}) %all-gather.6.cloned.1.call-update) | async-done | bytes 1179664 | tf_op jit(solution)/shard_map/all_gather | solution.py:104
  287.0 29.4 %all_to_all.60 = bf16[4,160,768]{2,1,0:T(8,128)(2,1)S(1)} all-to-all(bf16[4,160,768]{2,1,0:T(8,128)(2,1)} %bitcast.902), channel_id=1, replica_groups=mesh['section'=2,'dp'=4,'tensor'=4] {'dp'}, dimensions={0} | all-to-all | bytes 1966080 | tf_op jit(solution)/shard_map/all_to_all | solution.py:64
  326.8 33.4 %all_gather.94 = bf16[1,768,8]{2,0,1:T(2,128)(2,1)} all-gather(bf16[1,48,8]{2,0,1:T(2,128)(2,1)S(1)} %copy.219), channel_id=1, replica_groups=mesh['section'=2,'dp'=4,'tensor'=4] {'dp','tensor'}, dimensions={1}, use_global_device_ids=true | all-gather | bytes 13056 | tf_op jit(solution)/shard_map/all_gather | solution.py:109
  377.3 24.5 %reduce-scatter.42.cloned.1.call-done = f32[64,768]{1,0:T(8,128)} async-done(((f32[256,768]{1,0:T(8,128)}), f32[64,768]{1,0:T(8,128)}) %reduce-scatter.42.cloned.1.call-update) | async-done | bytes 196624 | tf_op jit(solution)/shard_map/reduce_scatter | solution.py:132
  454.8 22.4 %reduce-scatter.44.cloned.1.call-done = f32[64,768]{1,0:T(8,128)} async-done(((f32[256,768]{1,0:T(8,128)}), f32[64,768]{1,0:T(8,128)}) %reduce-scatter.44.cloned.1.call-update) | async-done | bytes 196624 | tf_op jit(solution)/shard_map/reduce_scatter | solution.py:132
  493.3 23.7 %reduce-scatter.46.cloned.1.call-done = f32[64,768]{1,0:T(8,128)} async-done(((f32[256,768]{1,0:T(8,128)}), f32[64,768]{1,0:T(8,128)}) %reduce-scatter.46.cloned.1.call-update) | async-done | bytes 196624 | tf_op jit(solution)/shard_map/reduce_scatter | solution.py:132
  534.3 29.6 %all_to_all.61 = bf16[4,160,768]{2,1,0:T(8,128)(2,1)S(1)} all-to-all(bf16[4,160,768]{2,1,0:T(8,128)(2,1)} %bitcast.903), channel_id=1, replica_groups=mesh['section'=2,'dp'=4,'tensor'=4] {'dp'}, dimensions={0} | all-to-all | bytes 1966080 | tf_op jit(solution)/shard_map/all_to_all | solution.py:64
  624.9 22.2 %all-to-all-done.6 = bf16[4,160,768]{2,1,0:T(8,128)(2,1)} async-done(((bf16[4,160,768]{2,1,0:T(8,128)(2,1)}), bf16[4,160,768]{2,1,0:T(8,128)(2,1)}, u32[]{:S(2)}, u32[]{:S(2)}) %all-to-all-start.6) | async-done | bytes 983072 | tf_op jit(solution)/shard_map/all_to_all | solution.py:64
  814.6 21.5 %reduce-scatter.50.cloned.1.call-done = f32[64,768]{1,0:T(8,128)} async-done(((f32[256,768]{1,0:T(8,128)}), f32[64,768]{1,0:T(8,128)}) %reduce-scatter.50.cloned.1.call-update) | async-done | bytes 196624 | tf_op jit(solution)/shard_map/reduce_scatter | solution.py:132
  836.1 25.9 %reduce-scatter.62.cloned.1.call-done = f32[64,768]{1,0:T(8,128)} async-done(((f32[256,768]{1,0:T(8,128)}), f32[64,768]{1,0:T(8,128)}) %reduce-scatter.62.cloned.1.call-update) | async-done | bytes 196624 | tf_op jit(solution)/shard_map/reduce_scatter | solution.py:132
  880.0 23.1 %reduce-scatter.52.cloned.1.call-done = f32[64,768]{1,0:T(8,128)} async-done(((f32[256,768]{1,0:T(8,128)}), f32[64,768]{1,0:T(8,128)}) %reduce-scatter.52.cloned.1.call-update) | async-done | bytes 196624 | tf_op jit(solution)/shard_map/reduce_scatter | solution.py:132
  921.6 29.4 %all_to_all.62 = bf16[4,160,768]{2,1,0:T(8,128)(2,1)S(1)} all-to-all(bf16[4,160,768]{2,1,0:T(8,128)(2,1)} %bitcast.904), channel_id=1, replica_groups=mesh['section'=2,'dp'=4,'tensor'=4] {'dp'}, dimensions={0} | all-to-all | bytes 1966080 | tf_op jit(solution)/shard_map/all_to_all | solution.py:64
  1003.7 28.1 %all_to_all.63 = bf16[4,160,768]{2,1,0:T(8,128)(2,1)S(1)} all-to-all(bf16[4,160,768]{2,1,0:T(8,128)(2,1)} %bitcast.901), channel_id=1, replica_groups=mesh['section'=2,'dp'=4,'tensor'=4] {'dp'}, dimensions={0} | all-to-all | bytes 1966080 | tf_op jit(solution)/shard_map/all_to_all | solution.py:64
  1042.2 23.6 %all-to-all-done.9 = bf16[4,160,768]{2,1,0:T(8,128)(2,1)} async-done(((bf16[4,160,768]{2,1,0:T(8,128)(2,1)}), bf16[4,160,768]{2,1,0:T(8,128)(2,1)}, u32[]{:S(2)}, u32[]{:S(2)}) %all-to-all-start.9) | async-done | bytes 983072 | tf_op jit(solution)/shard_map/all_to_all | solution.py:68
  1163.7 21.0 %reduce-scatter.68.cloned.1.call-done = bf16[256,384]{0,1:T(8,128)(2,1)} async-done(((bf16[1024,384]{0,1:T(8,128)(2,1)}), bf16[256,384]{0,1:T(8,128)(2,1)}) %reduce-scatter.68.cloned.1.call-update) | async-done | bytes 196624 | tf_op jit(solution)/shard_map/reduce_scatter | solution.py:419
  1188.9 22.9 %reduce-scatter.70.cloned.1.call-done = f32[64,768]{1,0:T(8,128)} async-done(((f32[256,768]{1,0:T(8,128)}), f32[64,768]{1,0:T(8,128)}) %reduce-scatter.70.cloned.1.call-update) | async-done | bytes 196624 | tf_op jit(solution)/shard_map/reduce_scatter | solution.py:132
  1245.4 29.6 %all_to_all.64 = bf16[4,160,768]{2,1,0:T(8,128)(2,1)S(1)} all-to-all(bf16[4,160,768]{2,1,0:T(8,128)(2,1)} %bitcast.900), channel_id=1, replica_groups=mesh['section'=2,'dp'=4,'tensor'=4] {'dp'}, dimensions={0} | all-to-all | bytes 1966080 | tf_op jit(solution)/shard_map/all_to_all | solution.py:64
  1285.6 23.2 %all-to-all-done.11 = bf16[4,160,768]{2,1,0:T(8,128)(2,1)} async-done(((bf16[4,160,768]{2,1,0:T(8,128)(2,1)}), bf16[4,160,768]{2,1,0:T(8,128)(2,1)}, u32[]{:S(2)}, u32[]{:S(2)}) %all-to-all-start.11) | async-done | bytes 983072 | tf_op jit(solution)/shard_map/all_to_all | solution.py:68
  1567.9 85.7 %all-reduce.4.cloned.1.call-done = bf16[1,2,768,768]{3,1,0,2:T(2,128)(2,1)} async-done(((bf16[1,2,768,768]{3,1,0,2:T(2,128)(2,1)}), bf16[1,2,768,768]{3,1,0,2:T(2,128)(2,1)}) %all-reduce.4.cloned.1.call-update) | async-done | bytes 2359312
  1656.2 27.9 %reduce-scatter.84.cloned.1.call-done = bf16[192,768]{1,0:T(8,128)(2,1)} async-done(((bf16[768,768]{1,0:T(8,128)(2,1)}), bf16[192,768]{1,0:T(8,128)(2,1)}) %reduce-scatter.84.cloned.1.call-update) | async-done | bytes 294928
  1689.6 52.2 %reduce-scatter.86.cloned.1.call-done = f32[48,3]{1,0:T(8,128)} async-done(((f32[768,3]{1,0:T(8,128)}), f32[48,3]{1,0:T(8,128)}) %reduce-scatter.86.cloned.1.call-update) | async-done | bytes 592
  1743.4 26.1 %reduce-scatter.80.cloned.1.call-done = bf16[192,576]{1,0:T(8,128)(2,1)} async-done(((bf16[768,576]{1,0:T(8,128)(2,1)}), bf16[192,576]{1,0:T(8,128)(2,1)}) %reduce-scatter.80.cloned.1.call-update) | async-done | bytes 221200
  (1035 shorter events, 1054.0 us)
Async XLA Ops:
  8.0 177.6 %reduce-scatter.38.cloned.1.call-start = ((), (), s32[]{:S(2)}) async-start(), calls=%async_computation.38 | async-start | bytes 983040 | tf_op jit(solution)/shard_map/reduce_scatter | solution.py:132
  163.6 81.2 %all-gather.6.cloned.1.call-start = ((), (), s32[]{:S(2)}) async-start(), calls=%async_computation.40 | async-start | bytes 1474560 | tf_op jit(solution)/shard_map/all_gather | solution.py:104
  164.2 106.6 %reduce-scatter.40.cloned.1.call-start = ((), (), s32[]{:S(2)}) async-start(), calls=%async_computation.41 | async-start | bytes 983040 | tf_op jit(solution)/shard_map/reduce_scatter | solution.py:132
  326.7 75.2 %reduce-scatter.42.cloned.1.call-start = ((), (), s32[]{:S(2)}) async-start(), calls=%async_computation.42 | async-start | bytes 983040 | tf_op jit(solution)/shard_map/reduce_scatter | solution.py:132
  377.3 99.9 %reduce-scatter.44.cloned.1.call-start = ((), (), s32[]{:S(2)}) async-start(), calls=%async_computation.43 | async-start | bytes 983040 | tf_op jit(solution)/shard_map/reduce_scatter | solution.py:132
  454.7 62.3 %reduce-scatter.46.cloned.1.call-start = ((), (), s32[]{:S(2)}) async-start(), calls=%async_computation.44 | async-start | bytes 983040 | tf_op jit(solution)/shard_map/reduce_scatter | solution.py:132
  658.0 65.3 %reduce-scatter.56.cloned.1.call-start = ((), (), s32[]{:S(2)}) async-start(), calls=%async_computation.49 | async-start | bytes 983040 | tf_op jit(solution)/shard_map/reduce_scatter | solution.py:132
  698.9 68.2 %reduce-scatter.58.cloned.1.call-start = ((), (), s32[]{:S(2)}) async-start(), calls=%async_computation.50 | async-start | bytes 983040 | tf_op jit(solution)/shard_map/reduce_scatter | solution.py:132
  737.8 72.5 %reduce-scatter.60.cloned.1.call-start = ((), (), s32[]{:S(2)}) async-start(), calls=%async_computation.51 | async-start | bytes 983040 | tf_op jit(solution)/shard_map/reduce_scatter | solution.py:419
  794.7 67.3 %reduce-scatter.62.cloned.1.call-start = ((), (), s32[]{:S(2)}) async-start(), calls=%async_computation.52 | async-start | bytes 983040 | tf_op jit(solution)/shard_map/reduce_scatter | solution.py:132
  814.5 88.5 %reduce-scatter.52.cloned.1.call-start = ((), (), s32[]{:S(2)}) async-start(), calls=%async_computation.47 | async-start | bytes 983040 | tf_op jit(solution)/shard_map/reduce_scatter | solution.py:132
  1041.9 61.9 %reduce-scatter.64.cloned.1.call-start = ((), (), s32[]{:S(2)}) async-start(), calls=%async_computation.53 | async-start | bytes 983040 | tf_op jit(solution)/shard_map/reduce_scatter | solution.py:132
  1082.9 58.8 %reduce-scatter.66.cloned.1.call-start = ((), (), s32[]{:S(2)}) async-start(), calls=%async_computation.54 | async-start | bytes 983040 | tf_op jit(solution)/shard_map/reduce_scatter | solution.py:132
  1118.0 66.7 %reduce-scatter.68.cloned.1.call-start = ((), (), s32[]{:S(2)}) async-start(), calls=%async_computation.55 | async-start | bytes 983040 | tf_op jit(solution)/shard_map/reduce_scatter | solution.py:419
  1285.0 61.7 %reduce-scatter.72.cloned.1.call-start = ((), (), s32[]{:S(2)}) async-start(), calls=%async_computation.57 | async-start | bytes 983040 | tf_op jit(solution)/shard_map/reduce_scatter | solution.py:132
  1360.5 78.1 %reduce-scatter.76.cloned.1.call-start = ((), (), s32[]{:S(2)}) async-start(), calls=%async_computation.59 | async-start | bytes 983040 | tf_op jit(solution)/shard_map/reduce_scatter | solution.py:419
  1403.1 83.1 %reduce-scatter.88.cloned.1.call-start = ((), (), s32[]{:S(2)}) async-start(), calls=%async_computation.65 | async-start | bytes 417792
  1418.4 98.2 %reduce-scatter.54.cloned.1.call-start = ((), (), s32[]{:S(2)}) async-start(), calls=%async_computation.48 | async-start | bytes 983040 | tf_op jit(solution)/shard_map/reduce_scatter | solution.py:132
  1423.4 112.2 %reduce-scatter.78.cloned.1.call-start = ((), (), s32[]{:S(2)}) async-start(), calls=%async_computation.60 | async-start | bytes 983040 | tf_op jit(solution)/shard_map/reduce_scatter | solution.py:132
  1442.9 123.2 %reduce-scatter.82.cloned.1.call-start = ((), (), s32[]{:S(2)}) async-start(), calls=%async_computation.62 | async-start | bytes 491520
  1457.0 196.7 %all-reduce.4.cloned.1.call-start = ((), (), s32[]{:S(2)}) async-start(), calls=%async_computation.66 | async-start | bytes 4718592
  1471.1 213.0 %reduce-scatter.84.cloned.1.call-start = ((), (), s32[]{:S(2)}) async-start(), calls=%async_computation.63 | async-start | bytes 1474560
  1508.3 233.6 %reduce-scatter.86.cloned.1.call-start = ((), (), s32[]{:S(2)}) async-start(), calls=%async_computation.64 | async-start | bytes 417792
  1542.0 227.5 %reduce-scatter.80.cloned.1.call-start = ((), (), s32[]{:S(2)}) async-start(), calls=%async_computation.61 | async-start | bytes 1228800
  (276 other events, 3983.4 us)
Sparse Core Ops, SparseCore 0:
  163.1 22.5 reduce-scatter.37
  248.2 22.4 reduce-scatter.39
  377.4 24.4 reduce-scatter.41
  454.8 22.2 reduce-scatter.43
  493.4 23.5 reduce-scatter.45
  627.1 23.7 reduce-scatter.47
  699.1 21.4 reduce-scatter.55
  737.9 21.7 reduce-scatter.57
  1118.1 23.5 reduce-scatter.65
  1189.0 22.7 reduce-scatter.69
  1360.6 23.5 reduce-scatter.73
Sparse Core Ops, SparseCore 1:
  165.1 49.2 all-gather.3
  215.9 28.8 all-gather.5
  789.8 20.4 reduce-scatter.59
  813.4 22.7 reduce-scatter.49
  838.8 23.2 reduce-scatter.61
  880.1 23.0 reduce-scatter.51
  1083.0 20.6 reduce-scatter.63
  1161.3 23.3 reduce-scatter.67
  1326.0 20.6 reduce-scatter.71
  1403.1 23.3 reduce-scatter.75
  1429.8 55.1 reduce-scatter.87
  1487.7 22.2 reduce-scatter.53
  1512.3 23.2 reduce-scatter.77
  1538.0 20.6 reduce-scatter.81
  1561.0 92.6 all-reduce.3
  1655.9 28.1 reduce-scatter.83
  1687.6 54.2 reduce-scatter.85
  1744.3 25.1 reduce-scatter.79
where the time goes:
time: 1790 us; the launch traced here: 1780 us
  waiting for transfers between devices  647 us (36%)
  blocking collectives  445 us (25%)
  local copies, waits for them, and re-layouts  249 us (14%)
  matrix products  208 us (12%)
  other arithmetic  167 us (9%)
  starting transfers between devices  42.3 us (2%)
  between operations  20.4 us (1%)
    reduce_scatter x18, waiting for transfers between devices, rows_out(): return lax.psum_scatter(part, 'tensor', scatter_dimension=0, tiled=True)  267 us
    unnamed x35, waiting for transfers between devices  193 us
    all_to_all x5, blocking collectives, send_rows(): return lax.all_to_all(part, 'dp', split_axis=0, concat_axis=0, tiled=True)  146 us
    all_gather x18, blocking collectives, rows_in(): return lax.all_gather(part, 'tensor', axis=0, tiled=True)  114 us
    all_to_all x6, waiting for transfers between devices, send_results(): lax.all_to_all(part.astype(jnp.bfloat16), 'dp', split_axis=0, concat_axis...  68.6 us
    unnamed x548, local copies, waits for them, and re-layouts  63.8 us
    all_gather x3, blocking collectives, on_device(): lax.all_gather(jnp.concatenate([projected[1], projected[2]], axis=1), 'dp...  55.2 us
    dynamic_update_slice x6, local copies, waits for them, and re-layouts, score_rows(): lax.dynamic_update_slice_in_dim(scores, near_scores, window_start, 2)  49.8 us
  transfers between devices with their start and end apart: 40, of which 32 were waited for; matrix products, arithmetic and copies ran while one was open for 15% of the time, Pallas kernels for 0%

commit v1 on v0

v1 whole, which is shorter than its diff:
```python
import jax
import jax.numpy as jnp
import numpy as np
from jax import lax
from jax.experimental import pallas as pl
from jax.experimental.pallas import tpu as pltpu
from jax.sharding import PartitionSpec as P

HD = 64
NB = 32
MAXDIST = 128


highest_precision = lax.Precision.HIGHEST
norm_eps = 1e-06
masked_score = -1000000000.0


def from_behind(value, axis, steps):
    count = lax.axis_size(axis)
    first, last = (max(0, -steps), min(count, count - steps))
    return lax.ppermute(value, axis, [(source, source + steps) for source in range(first, last)])


def bucket_edges():
    exact_span = NB // 2
    distance = np.arange(1, 4 * MAXDIST + 1) * 1.0
    log_ratio = np.log(np.maximum(distance, exact_span) / exact_span) / np.log(MAXDIST / exact_span)
    far_bucket = np.minimum(exact_span + np.floor(log_ratio * (NB - exact_span)), NB - 1)
    bucket = np.where(distance < exact_span, distance, far_bucket)
    return [int(distance[np.argmax(bucket >= bucket_no)]) for bucket_no in range(1, NB)]


def relative_bucket(distance):
    bucket = jnp.zeros(distance.shape, jnp.int32)
    for edge_at in bucket_edges():
        bucket = bucket + (distance >= edge_at).astype(jnp.int32)
    return bucket


def norm_rows(hidden_in, gain_row):
    return (
        hidden_in
        * lax.rsqrt(jnp.mean(hidden_in * hidden_in, axis=-1, keepdims=True) + norm_eps)
        * gain_row
    )


def gelu_tanh(inputs):
    return jax.nn.gelu(inputs, approximate=True)


def gated(gate_part, up_part):
    return gelu_tanh(gate_part) * up_part


def gate_weights(logits, route_rows):
    chosen = route_rows[:, :, None] == jnp.arange(logits.shape[1], dtype=jnp.int32)[None, None, :]
    picked = jnp.sum(jnp.where(chosen, logits[:, None, :], 0.0), axis=2)
    row_max = jnp.max(picked, axis=1, keepdims=True)
    raised = jnp.exp(picked - row_max)
    return (raised / jnp.sum(raised, axis=1, keepdims=True), chosen)


VMEM_BYTES = 24 << 20


def whole_specs(count):
    return [pl.BlockSpec(memory_space=pltpu.VMEM)] * count


def push(source, target, sent, landed, device):
    copy = pltpu.make_async_remote_copy(
        src_ref=source,
        dst_ref=target,
        send_sem=sent,
        recv_sem=landed,
        device_id=device,
        device_id_type=pl.DeviceIdType.MESH,
    )
    copy.start()
    return copy


def greet(axis_counts):
    barrier = pltpu.get_barrier_semaphore()
    total = 0
    for axis, count in axis_counts:
        me = lax.axis_index(axis)
        for step in range(1, count):
            pl.semaphore_signal(
                barrier,
                inc=1,
                device_id={axis: lax.rem(me + step, count)},
                device_id_type=pl.DeviceIdType.MESH,
            )
        total += count - 1
    pl.semaphore_wait(barrier, total)


def sum_kernel(count, backward, gather, *refs):
    refs = list(refs)
    part_ref, base_ref = refs[:2]
    del refs[:2]
    if backward:
        value_ref = refs.pop(0)
    if backward or gather:
        gain_ref = refs.pop(0)
    new_ref = refs.pop(0)
    if backward:
        gain_grad_ref = refs.pop(0)
    if gather:
        rows_ref = refs.pop(0)
    out_buf, in_buf, sent, landed = refs[:4]
    me = lax.axis_index("tensor")
    greet([("tensor", count)])
    copies = []
    for step in range(1, count):
        peer = lax.rem(me + step, count)
        out_buf[step - 1] = part_ref[peer].astype(jnp.bfloat16)
        copies.append(
            push(
                out_buf.at[step - 1],
                in_buf.at[step - 1],
                sent.at[step - 1],
                landed.at[step - 1],
                {"tensor": peer},
            )
        )
    total = part_ref[me]
    if not backward:
        total = total + base_ref[...]
    for step in range(1, count):
        copies[step - 1].wait_recv()
        total = total + in_buf[step - 1].astype(jnp.float32)
    if backward:
        value = value_ref[...]
        root = lax.rsqrt(jnp.mean(value * value, axis=-1, keepdims=True) + norm_eps)
        scaled = total * gain_ref[...]
        pull = jnp.mean(scaled * value, axis=-1, keepdims=True)
        gain_grad_ref[...] = jnp.sum(total * (value * root), axis=0, keepdims=True)
        new = base_ref[...] + (root * scaled - value * (root * root * root * pull))
        rounded = new
    else:
        new = total
        if gather:
            rounded = norm_rows(new, gain_ref[...])
    new_ref[...] = new
    if gather:
        sent2, landed2 = refs[4:]
        rows_ref[me] = rounded.astype(jnp.bfloat16)
        for step in range(1, count):
            copies.append(
                push(
                    rows_ref.at[me],
                    rows_ref.at[me],
                    sent2.at[step - 1],
                    landed2.at[step - 1],
                    {"tensor": lax.rem(me + step, count)},
                )
            )
        for copy in copies[count - 1 :]:
            copy.wait_recv()
    for copy in copies:
        copy.wait_send()


def sum_rows(part, base, value=None, gain=None, gather=True):
    backward = value is not None
    count = lax.axis_size("tensor")
    rows, model = base.shape
    args = [part.reshape(count, rows, model), base]
    out_shape = [jax.ShapeDtypeStruct((rows, model), jnp.float32)]
    if backward:
        args.append(value)
        out_shape.append(jax.ShapeDtypeStruct((1, model), jnp.float32))
    if backward or gather:
        args.append(gain[None])
    sems = [pltpu.SemaphoreType.DMA((count - 1,))] * 2
    if gather:
        out_shape.append(jax.ShapeDtypeStruct((count, rows, model), jnp.bfloat16))
        sems = sems * 2
    out = pl.pallas_call(
        lambda *refs: sum_kernel(count, backward, gather, *refs),
        out_shape=out_shape,
        in_specs=whole_specs(len(args)),
        out_specs=whole_specs(len(out_shape)),
        scratch_shapes=[pltpu.VMEM((count - 1, rows, model), jnp.bfloat16)] * 2 + sems,
        compiler_params=pltpu.CompilerParams(
            collective_id=2 * int(backward) + int(gather),
            has_side_effects=True,
            vmem_limit_bytes=VMEM_BYTES,
        ),
    )(*args)
    out = list(out)
    if gather:
        out[-1] = out[-1].reshape(count * rows, model)
    return out


def dispatch_kernel(dp_count, tensor_count, in_ref, out_ref, sent, landed, sent2, landed2):
    me, place = lax.axis_index("dp"), lax.axis_index("tensor")
    high, wide = in_ref.shape[1] // 2, in_ref.shape[2] // 2
    rows = pl.ds(pl.multiple_of((place // 2) * high, 16), high)
    columns = pl.ds(pl.multiple_of((place % 2) * wide, 128), wide)
    greet([("dp", dp_count), ("tensor", tensor_count)])
    first, second = [], []
    for step in range(1, dp_count):
        peer = lax.rem(me + step, dp_count)
        first.append(
            push(
                in_ref.at[peer, rows, columns],
                out_ref.at[me, rows, columns],
                sent.at[step - 1],
                landed.at[step - 1],
                {"dp": peer},
            )
        )
    out_ref[me] = in_ref[me]
    for step in range(1, dp_count):
        first[step - 1].wait_recv()
        source = lax.rem(me + dp_count - step, dp_count)
        for hop in range(1, tensor_count):
            index = (step - 1) * (tensor_count - 1) + hop - 1
            second.append(
                push(
                    out_ref.at[source, rows, columns],
                    out_ref.at[source, rows, columns],
                    sent2.at[index],
                    landed2.at[index],
                    {"tensor": lax.rem(place + hop, tensor_count)},
                )
            )
    for copy in first:
        copy.wait_send()
    for copy in second:
        copy.wait()


def send_rows(part):
    dp_count, tensor_count = lax.axis_size("dp"), lax.axis_size("tensor")
    hops = (dp_count - 1) * (tensor_count - 1)
    return pl.pallas_call(
        lambda *refs: dispatch_kernel(dp_count, tensor_count, *refs),
        out_shape=jax.ShapeDtypeStruct(part.shape, part.dtype),
        in_specs=whole_specs(1),
        out_specs=whole_specs(1)[0],
        scratch_shapes=[pltpu.SemaphoreType.DMA((dp_count - 1,))] * 2
        + [pltpu.SemaphoreType.DMA((hops,))] * 2,
        compiler_params=pltpu.CompilerParams(
            collective_id=4, has_side_effects=True, vmem_limit_bytes=VMEM_BYTES
        ),
    )(part)


def exchange_kernel(dp_count, in_ref, out_ref, sent, landed):
    me = lax.axis_index("dp")
    greet([("dp", dp_count)])
    copies = []
    for step in range(1, dp_count):
        peer = lax.rem(me + step, dp_count)
        copies.append(
            push(
                in_ref.at[peer],
                out_ref.at[me],
                sent.at[step - 1],
                landed.at[step - 1],
                {"dp": peer},
            )
        )
    out_ref[me] = in_ref[me]
    for copy in copies:
        copy.wait()


def send_results(part):
    dp_count = lax.axis_size("dp")
    part = part.astype(jnp.bfloat16)
    return pl.pallas_call(
        lambda *refs: exchange_kernel(dp_count, *refs),
        out_shape=jax.ShapeDtypeStruct(part.shape, part.dtype),
        in_specs=whole_specs(1),
        out_specs=whole_specs(1)[0],
        scratch_shapes=[pltpu.SemaphoreType.DMA((dp_count - 1,))] * 2,
        compiler_params=pltpu.CompilerParams(
            collective_id=5, has_side_effects=True, vmem_limit_bytes=VMEM_BYTES
        ),
    )(part)


def on_device(
    tokens,
    cotangent,
    w_qkv,
    w_out,
    w_gate_up,
    w_down,
    rel_table,
    gains,
    router,
    w_in,
    w_expert_out,
    routes,
):
    dp_count = lax.axis_size("dp")
    tensor_count = lax.axis_size("tensor")
    dp_place = lax.axis_index("dp")
    is_first = lax.axis_index("section") == 0
    micro_count = tokens.shape[0]
    local_rows = tokens.shape[1]
    model = tokens.shape[2]
    tok_dp = local_rows * tensor_count
    seq_span = min(4, dp_count)
    length = tok_dp * seq_span
    expert_count = router.shape[2]
    top_count = routes.shape[3]
    capacity = (5 * tok_dp * top_count + 4 * expert_count - 1) // (4 * expert_count)
    wide = w_qkv.shape[3]
    hidden_wide = w_gate_up.shape[3]
    attn_weight = lax.all_gather(
        jnp.concatenate([w_qkv[0, 0], w_qkv[0, 1], w_qkv[0, 2], w_out[0].T], axis=1),
        "dp",
        axis=0,
        tiled=True,
    )
    mlp_weight = lax.all_gather(
        jnp.concatenate([w_gate_up[0, 0], w_gate_up[0, 1], w_down[0].T], axis=1),
        "dp",
        axis=0,
        tiled=True,
    )
    qkv_weight = attn_weight[:, : 3 * wide]
    out_weight = attn_weight[:, 3 * wide :]
    gate_up_weight = mlp_weight[:, : 2 * hidden_wide]
    down_weight = mlp_weight[:, 2 * hidden_wide :]
    gain_size, small_size = gains[0].size, gains[0].size + router[0].size
    table_rows, heads_here = rel_table.shape[1:]
    packed = jnp.concatenate([gains[0].reshape(-1), router[0].reshape(-1), rel_table[0].reshape(-1)])
    packed_size = packed.size
    packed = jnp.pad(packed, (0, -packed_size % 1024))
    small_all = lax.all_gather(packed, ("dp", "tensor"), axis=0, tiled=False)
    gain_all = (
        small_all[:, :gain_size]
        .reshape(-1, gains.shape[1], gains.shape[2])
        .transpose(1, 0, 2)
        .reshape(gains.shape[1], model)
        .astype(jnp.float32)
    )
    router_all = small_all[:, gain_size:small_size].reshape(model, router.shape[2])
    table_low = lax.dynamic_index_in_dim(
        small_all[:, small_size:packed_size].reshape(dp_count, tensor_count, table_rows, heads_here),
        lax.axis_index("tensor"),
        1,
        keepdims=False,
    ).reshape(dp_count * table_rows, heads_here)
    position_table = table_low.astype(jnp.float32)
    router_wide = router_all.astype(jnp.float32)
    inner_weight = w_in[0]
    outer_weight = w_expert_out[0]
    head_count = position_table.shape[1]
    head_width = head_count * HD
    seq_start = dp_place // seq_span * length
    seq_place = dp_place % seq_span
    own_experts = expert_count // dp_count
    used_rows = own_experts * capacity
    block_rows = -(-used_rows // 32) * 32
    scale = HD ** (-0.5)

    def rows_in(part):
        return lax.all_gather(part, "tensor", axis=0, tiled=True)

    window = min(length, tok_dp + MAXDIST)
    distance = (
        jnp.arange(tok_dp, dtype=jnp.int32)[:, None]
        - (jnp.arange(length, dtype=jnp.int32) - (length - tok_dp))[None, :]
    )
    near_bucket = relative_bucket(distance[:, length - window :])
    one_hot_matrix = (
        near_bucket[None, :, :] == jnp.arange(NB, dtype=jnp.int32)[:, None, None]
    ).astype(jnp.bfloat16)
    nearby_bias = jnp.einsum(
        "vod,vl->lod", one_hot_matrix, table_low, preferred_element_type=jnp.float32
    )
    far_bias = jnp.broadcast_to(
        position_table[NB - 1][:, None, None], (head_count, tok_dp, length - window)
    )
    first_key = (seq_span - 1 - seq_place) * tok_dp
    allowed = (distance >= 0) & (jnp.arange(length, dtype=jnp.int32)[None, :] >= first_key)
    bias = jnp.where(allowed[None], jnp.concatenate([far_bias, nearby_bias], axis=2), masked_score)

    def score_rows(queries, key_rows):
        raw_scores = jnp.einsum(
            "qhd,khd->hqk", queries, key_rows, preferred_element_type=jnp.float32
        )
        return raw_scores * scale + bias

    def slot_matrix(slot_ids):
        slots = jnp.arange(dp_count * block_rows, dtype=jnp.int32)
        return slots[:, None, None] == slot_ids.reshape(tok_dp, top_count).T[None]

    def to_blocks(hits, rows):
        place = jnp.any(hits, axis=1).astype(jnp.bfloat16)
        return jnp.dot(place, rows, preferred_element_type=jnp.float32).astype(jnp.bfloat16)

    def from_blocks(hits, returned):
        flat_rows = returned.reshape(-1, model)
        return jnp.stack(
            [
                jnp.einsum(
                    "st,sd->td",
                    hits[:, top_no].astype(jnp.bfloat16),
                    flat_rows,
                    preferred_element_type=jnp.float32,
                )
                for top_no in range(top_count)
            ],
            axis=1,
        )

    def expert_blocks(rows):
        return rows[:, :used_rows].reshape(dp_count, own_experts, capacity, model)

    def dp_blocks(rows):
        rows = rows.reshape(dp_count, used_rows, model).astype(jnp.bfloat16)
        return jnp.pad(rows, ((0, 0), (0, block_rows - used_rows), (0, 0)))

    def attend_back(queries, pair_rows, log_total, grad_attended):
        key_count = pair_rows.shape[0]
        pairs = pair_rows.reshape(key_count, 2, head_count, HD)
        scores = score_rows(queries, pairs[:, 0])
        soft = jnp.exp(scores - log_total)
        grad_soft = jnp.einsum(
            "qhd,khd->hqk", grad_attended, pairs[:, 1], preferred_element_type=jnp.float32
        )
        inner_sum = jnp.sum(soft * grad_soft, axis=2, keepdims=True)
        grad_scores = (soft * (grad_soft - inner_sum)).astype(jnp.bfloat16)
        nearby_gradient = grad_scores[:, :, length - window :]
        table_gradient = jnp.einsum(
            "ptm,stm->ps", one_hot_matrix, nearby_gradient, preferred_element_type=jnp.float32
        )
        far_sum = jnp.sum(
            grad_scores[:, :, : length - window].astype(jnp.float32), axis=(1, 2)
        )
        table_gradient = table_gradient.at[NB - 1].add(far_sum)
        grad_queries = (
            jnp.einsum("hqk,khd->qhd", grad_scores, pairs[:, 0], preferred_element_type=jnp.float32)
            * scale
        )
        grad_keys = (
            jnp.einsum("hqk,qhd->khd", grad_scores, queries, preferred_element_type=jnp.float32)
            * scale
        )
        grad_values = jnp.einsum(
            "hqk,qhd->khd",
            soft.astype(jnp.bfloat16),
            grad_attended,
            preferred_element_type=jnp.float32,
        )
        grad_pairs = jnp.stack([grad_keys, grad_values], axis=1).reshape(key_count, 2 * head_width)
        return (grad_queries.reshape(tok_dp, head_width), grad_pairs, table_gradient)

    outputs = []
    kept_ticks = []
    arrived_rows = jnp.zeros_like(tokens[0])
    for tick_no in range(micro_count + 1):
        section_input = jnp.where(is_first, tokens[min(tick_no, micro_count - 1)], arrived_rows)
        route_rows = jnp.where(
            is_first, routes[0, min(tick_no, micro_count - 1)], routes[0, max(tick_no - 1, 0)]
        )
        forward_residual = section_input.astype(jnp.float32)
        forward_rows_attn = rows_in(norm_rows(forward_residual, gain_all[0]).astype(jnp.bfloat16))
        projected = jnp.dot(
            forward_rows_attn, qkv_weight, preferred_element_type=jnp.float32
        ).astype(jnp.bfloat16)
        forward_queries = projected[:, :head_width].reshape(tok_dp, head_count, HD)
        everything = lax.all_gather(projected[:, head_width:], "dp", axis=0, tiled=True)
        fetched = lax.dynamic_slice_in_dim(everything, seq_start, length, 0)
        fetched = lax.dynamic_slice_in_dim(
            jnp.concatenate([fetched, fetched]), (seq_place + 1) * tok_dp, length, 0
        )
        attend_pairs = fetched.reshape(fetched.shape[0], 2, head_count, HD)
        attend_scores = score_rows(forward_queries, attend_pairs[:, 0])
        row_max = jnp.max(attend_scores, axis=2, keepdims=True)
        attend_log_total = row_max + jnp.log(
            jnp.sum(jnp.exp(attend_scores - row_max), axis=2, keepdims=True)
        )
        attend_soft = jnp.exp(attend_scores - attend_log_total).astype(jnp.bfloat16)
        attend_attended = jnp.einsum(
            "hqk,khd->qhd", attend_soft, attend_pairs[:, 1], preferred_element_type=jnp.float32
        )
        forward_attended = attend_attended.reshape(tok_dp, head_width).astype(jnp.bfloat16)
        forward_residual1, forward_rows_mlp = sum_rows(
            jnp.einsum(
                "tf,df->td", forward_attended, out_weight, preferred_element_type=jnp.float32
            ),
            forward_residual,
            gain=gain_all[1],
        )
        forward_gate_up = jnp.dot(
            forward_rows_mlp, gate_up_weight, preferred_element_type=jnp.float32
        )
        forward_hidden = gated(
            forward_gate_up[:, :hidden_wide], forward_gate_up[:, hidden_wide:]
        ).astype(jnp.bfloat16)
        forward_residual2, forward_rows_moe = sum_rows(
            jnp.einsum(
                "tf,df->td", forward_hidden, down_weight, preferred_element_type=jnp.float32
            ),
            forward_residual1,
            gain=gain_all[2],
        )
        logits = jnp.dot(forward_rows_moe, router_all, preferred_element_type=jnp.float32)
        forward_gate_probs, forward_chosen = gate_weights(logits, route_rows)
        flat = route_rows.reshape(-1)
        expert_one_hot_matrix = (
            flat[:, None] == jnp.arange(expert_count, dtype=jnp.int32)[None, :]
        ).astype(jnp.bfloat16)
        pair_no = jnp.arange(tok_dp * top_count, dtype=jnp.int32)
        before = jnp.dot(
            (pair_no[:, None] > pair_no[None, :]).astype(jnp.bfloat16),
            expert_one_hot_matrix,
            preferred_element_type=jnp.float32,
        )
        forward_slot_ids = (
            flat // own_experts * block_rows
            + flat % own_experts * capacity
            + jnp.sum(before * expert_one_hot_matrix.astype(jnp.float32), axis=1).astype(jnp.int32)
        )
        forward_hits = slot_matrix(forward_slot_ids)
        forward_arrived = expert_blocks(
            send_rows(
                to_blocks(forward_hits, forward_rows_moe).reshape(dp_count, block_rows, model)
            )
        )
        forward_before_act = jnp.einsum(
            "secd,edf->secf", forward_arrived, inner_weight, preferred_element_type=jnp.float32
        )
        forward_active = gelu_tanh(forward_before_act).astype(jnp.bfloat16)
        results = jnp.einsum(
            "secf,efd->secd", forward_active, outer_weight, preferred_element_type=jnp.float32
        )
        returned = send_results(dp_blocks(results))
        forward_picked_rows = from_blocks(forward_hits, returned)
        residual3 = sum_rows(
            jnp.sum(forward_gate_probs[:, :, None] * forward_picked_rows, axis=1),
            forward_residual2,
            gather=False,
        )[0]
        forward_picked_rows = forward_picked_rows.astype(jnp.bfloat16)
        forward_kept = (
            forward_residual,
            forward_rows_attn,
            forward_queries,
            fetched,
            attend_log_total,
            forward_attended,
            forward_residual1,
            forward_rows_mlp,
            forward_gate_up,
            forward_hidden,
            forward_residual2,
            forward_rows_moe,
            forward_gate_probs,
            forward_chosen,
            forward_slot_ids,
            forward_picked_rows,
            forward_arrived,
            forward_before_act,
            forward_active,
        )
        result = residual3.astype(jnp.bfloat16)
        kept = forward_kept
        outputs.append(result)
        kept_ticks.append(kept)
        if tick_no < micro_count:
            arrived_rows = from_behind(result, "section", 1)
    grad_sums = (
        jnp.zeros(qkv_weight.shape, jnp.float32),
        jnp.zeros(out_weight.shape, jnp.float32),
        jnp.zeros(gate_up_weight.shape, jnp.float32),
        jnp.zeros(down_weight.shape, jnp.float32),
        jnp.zeros(position_table.shape, jnp.float32),
        jnp.zeros(gain_all.shape, jnp.float32),
        jnp.zeros(router_all.shape, jnp.float32),
        jnp.zeros(inner_weight.shape, jnp.float32),
        jnp.zeros(outer_weight.shape, jnp.float32),
    )
    returned_grad = jnp.zeros_like(tokens[0])
    input_list = []
    for tick_no in range(micro_count + 1):
        if tick_no < micro_count:
            outer_cot = cotangent[tick_no]
        else:
            outer_cot = jnp.zeros_like(cotangent[0])
        upstream = jnp.where(is_first, returned_grad, outer_cot)
        kept = jax.tree.map(
            lambda early, late: jnp.where(is_first, early, late),
            kept_ticks[max(tick_no - 1, 0)],
            kept_ticks[min(tick_no + 1, micro_count)],
        )
        (
            residual,
            rows_attn,
            backward_queries,
            backward_pair_rows,
            backward_log_total,
            attended,
            residual1,
            rows_mlp,
            gate_up,
            hidden,
            residual2,
            rows_moe,
            gate_probs,
            chosen,
            slot_ids,
            picked_rows,
            arrived,
            before_act,
            active,
        ) = kept
        grad3 = upstream.astype(jnp.float32)
        rows_grad3 = rows_in(upstream)
        wide_grad3 = rows_grad3.astype(jnp.float32)
        hits = slot_matrix(slot_ids)
        slot_gate = jnp.sum(
            jnp.where(hits, gate_probs.T[None], 0.0), axis=(1, 2)
        )
        slot_place = jnp.any(hits, axis=1).astype(jnp.bfloat16)
        outgoing = (
            jnp.dot(slot_place, rows_grad3, preferred_element_type=jnp.float32)
            * slot_gate[:, None]
        ).astype(jnp.bfloat16)
        grad_results = expert_blocks(send_rows(outgoing.reshape(dp_count, block_rows, model)))
        grad_gate = jnp.sum(wide_grad3[:, None, :] * picked_rows.astype(jnp.float32), axis=2)
        grad_active = jnp.einsum(
            "secd,efd->secf", grad_results, outer_weight, preferred_element_type=jnp.float32
        )
        outer_grad = jnp.einsum(
            "secf,secd->efd", active, grad_results, preferred_element_type=jnp.float32
        )
        gelu_back = jax.vjp(gelu_tanh, before_act)[1]
        grad_before = gelu_back(grad_active)[0].astype(jnp.bfloat16)
        inner_grad = jnp.einsum(
            "secd,secf->edf", arrived, grad_before, preferred_element_type=jnp.float32
        )
        grad_arrived = jnp.einsum(
            "secf,edf->secd", grad_before, inner_weight, preferred_element_type=jnp.float32
        )
        grad_back = send_results(dp_blocks(grad_arrived))
        grad_copies = jnp.einsum(
            "st,sd->td",
            slot_place,
            grad_back.reshape(-1, model),
            preferred_element_type=jnp.float32,
        )
        grad_picked = gate_probs * (
            grad_gate - jnp.sum(gate_probs * grad_gate, axis=1, keepdims=True)
        )
        grad_logits = jnp.sum(jnp.where(chosen, grad_picked[:, :, None], 0.0), axis=1)
        router_grad = jnp.dot(
            rows_moe.astype(jnp.float32).T, grad_logits, precision=highest_precision
        )
        grad_moe_rows = grad_copies + jnp.dot(
            grad_logits, router_wide.T, precision=highest_precision
        )
        grad2, gain_grad2, rows_grad2 = sum_rows(
            grad_moe_rows, grad3, residual2, gain_all[2]
        )
        grad_hidden = jnp.dot(rows_grad2, down_weight, preferred_element_type=jnp.float32)
        down_grad = jnp.einsum("td,tf->df", rows_grad2, hidden, preferred_element_type=jnp.float32)
        gated_back = jax.vjp(gated, gate_up[:, :hidden_wide], gate_up[:, hidden_wide:])[1]
        grad_gate_up = jnp.concatenate(gated_back(grad_hidden), axis=1).astype(jnp.bfloat16)
        gate_up_grad = jnp.einsum(
            "td,tf->df", rows_mlp, grad_gate_up, preferred_element_type=jnp.float32
        )
        grad_mid = jnp.einsum(
            "tf,df->td", grad_gate_up, gate_up_weight, preferred_element_type=jnp.float32
        )
        grad1, gain_grad1, rows_grad1 = sum_rows(grad_mid, grad2, residual1, gain_all[1])
        backward_grad_attended = jnp.dot(
            rows_grad1, out_weight, preferred_element_type=jnp.float32
        ).astype(jnp.bfloat16)
        output_gradient = jnp.einsum(
            "td,tf->df", rows_grad1, attended, preferred_element_type=jnp.float32
        )
        backward_grad_queries, backward_grad_pairs, backward_table_gradient = attend_back(
            backward_queries,
            backward_pair_rows,
            backward_log_total,
            backward_grad_attended.reshape(tok_dp, head_count, HD),
        )
        low_pairs = backward_grad_pairs.astype(jnp.bfloat16)
        spread_rows = lax.dynamic_slice_in_dim(
            jnp.concatenate([low_pairs, low_pairs]), first_key, length, 0
        )
        if dp_count > seq_span:
            spread_rows = lax.dynamic_update_slice_in_dim(
                jnp.zeros((dp_count * tok_dp, 2 * head_width), jnp.bfloat16),
                spread_rows,
                seq_start,
                0,
            )
        own_rows = lax.psum_scatter(spread_rows, "dp", scatter_dimension=0, tiled=True)
        grad_project = jnp.concatenate(
            [backward_grad_queries.astype(jnp.bfloat16), own_rows], axis=1
        )
        qkv_grad = jnp.einsum(
            "td,tf->df", rows_attn, grad_project, preferred_element_type=jnp.float32
        )
        grad0, gain_grad0 = sum_rows(
            jnp.einsum(
                "tf,df->td", grad_project, qkv_weight, preferred_element_type=jnp.float32
            ),
            grad1,
            residual,
            gain_all[0],
            gather=False,
        )
        gain_grad = jnp.concatenate([gain_grad0, gain_grad1, gain_grad2])
        step_grads = (
            qkv_grad,
            output_gradient,
            gate_up_grad,
            down_grad,
            backward_table_gradient,
            gain_grad,
            router_grad,
            inner_grad,
            outer_grad,
        )
        grad_input, step_grads = (grad0.astype(jnp.bfloat16), step_grads)
        grad_sums = jax.tree.map(jnp.add, grad_sums, step_grads)
        input_list.append(grad_input)
        if tick_no < micro_count:
            returned_grad = from_behind(grad_input, "section", -1)
    block_out = jnp.stack(
        [
            jnp.where(is_first, outputs[micro_no], outputs[micro_no + 1])
            for micro_no in range(micro_count)
        ]
    )[None]
    input_grads = jnp.stack(
        [
            jnp.where(is_first, input_list[micro_no + 1], input_list[micro_no])
            for micro_no in range(micro_count)
        ]
    )[None]
    mlp_grads = lax.psum_scatter(
        jnp.concatenate([grad_sums[2], grad_sums[3]], axis=1).astype(jnp.bfloat16),
        "dp",
        scatter_dimension=0,
        tiled=True,
    ).astype(jnp.float32)
    attn_grads = lax.psum_scatter(
        jnp.concatenate([grad_sums[0], grad_sums[1]], axis=1).astype(jnp.bfloat16),
        "dp",
        scatter_dimension=0,
        tiled=True,
    ).astype(jnp.float32)
    devices = dp_count * tensor_count
    is_mine = jnp.arange(tensor_count) == lax.axis_index("tensor")
    table_shares = jnp.where(
        is_mine[None, :, None], grad_sums[4].reshape(dp_count, 1, table_rows * heads_here), 0.0
    )
    small = jnp.concatenate(
        [
            grad_sums[5]
            .reshape(gains.shape[1], devices, gains.shape[2])
            .transpose(1, 0, 2)
            .reshape(devices, -1),
            grad_sums[6].reshape(devices, -1),
            table_shares.reshape(devices, -1),
        ],
        axis=1,
    )
    small = jnp.pad(small, ((0, 0), (0, -packed_size % 1024)))
    small = lax.psum_scatter(small, ("dp", "tensor"), scatter_dimension=0, tiled=False)
    return (
        block_out,
        input_grads,
        jnp.stack([attn_grads[:, part * wide : (part + 1) * wide] for part in range(3)])[None],
        attn_grads[:, 3 * wide :].T[None],
        jnp.stack([mlp_grads[:, :hidden_wide], mlp_grads[:, hidden_wide : 2 * hidden_wide]])[None],
        mlp_grads[:, 2 * hidden_wide :].T[None],
        small[small_size:packed_size].reshape(1, table_rows, heads_here),
        small[:gain_size].reshape(1, gains.shape[1], gains.shape[2]),
        small[gain_size:small_size].reshape(1, router.shape[1], router.shape[2]),
        grad_sums[7][None],
        grad_sums[8][None],
    )


def solution(mesh):
    placed = (
        P(None, ("dp", "tensor"), None),
        P(None, ("dp", "tensor"), None),
        P("section", None, "dp", "tensor"),
        P("section", "tensor", "dp"),
        P("section", None, "dp", "tensor"),
        P("section", "tensor", "dp"),
        P("section", "dp", "tensor"),
        P("section", None, ("dp", "tensor")),
        P("section", ("dp", "tensor"), None),
        P("section", "dp", None, "tensor"),
        P("section", "dp", "tensor", None),
        P("section", None, "dp", None),
    )
    return jax.shard_map(
        on_device,
        mesh=mesh,
        in_specs=placed,
        out_specs=(
            P("section", None, ("dp", "tensor"), None),
            P("section", None, ("dp", "tensor"), None),
            P("section", None, "dp", "tensor"),
            P("section", "tensor", "dp"),
            P("section", None, "dp", "tensor"),
            P("section", "tensor", "dp"),
            P("section", "dp", "tensor"),
            P("section", None, ("dp", "tensor")),
            P("section", ("dp", "tensor"), None),
            P("section", "dp", None, "tensor"),
            P("section", "dp", "tensor", None),
        ),
        check_vma=False,
    )
```

time: 1790 us -> 1080 us (0.60)
  waiting for transfers between devices: 647 us -> 148 us
  Pallas kernels: 0 us -> 420 us
  blocking collectives: 445 us -> 140 us
  local copies, waits for them, and re-layouts: 249 us -> 96.5 us
  other arithmetic: 167 us -> 76.1 us
  matrix products: 208 us -> 156 us
  starting transfers between devices: 42.3 us -> 10.6 us
    pallas_call x0 -> x30, Pallas kernels: none -> 420 us  [the longest x18 179 us: sum_rows(): pl.pallas_call(lambda *refs: sum_kernel(count, backward, gather, *refs),...]
    reduce_scatter x21 -> x4, waiting for transfers between devices: 301 us -> 65.2 us  [the longest x1 64.5 us: on_device(): lax.psum_scatter(jnp.concatenate([grad_sums[2], grad_sums[3]], axis=1).as...]
    all_to_all x5 -> x0, blocking collectives: 146 us -> none  [send_rows(): return lax.all_to_all(part, 'dp', split_axis=0, concat_axis=0, tiled=True)]
    unnamed x35 -> x10, waiting for transfers between devices: 193 us -> 73 us
    all_to_all x7 -> x0, waiting for transfers between devices: 90.8 us -> none  [the longest x6 68.6 us: send_results(): lax.all_to_all(part.astype(jnp.bfloat16), 'dp', split_axis=0, concat_axis...]
    all_gather x18 -> x6, blocking collectives: 114 us -> 39.1 us  [rows_in(): return lax.all_gather(part, 'tensor', axis=0, tiled=True)]
    all_gather x8 -> x4, blocking collectives: 174 us -> 100 us  [the longest x3 77 us: on_device(): lax.all_gather(projected[:, head_width:], 'dp', axis=0, tiled=True)]
    dynamic_update_slice x6 -> x0, local copies, waits for them, and re-layouts: 49.8 us -> none  [score_rows(): lax.dynamic_update_slice_in_dim(scores, near_scores, window_start, 2)]
  transfers between devices with their start and end apart: 40 -> 12, of which waited for: 32 -> 7; matrix products, arithmetic and copies ran while one was open for 15% -> 18% of each run, Pallas kernels for 0% -> 8%
where the time goes in v1:
time: 1080 us; the launch traced here: 1060 us
  Pallas kernels  420 us (39%)
  matrix products  156 us (14%)
  waiting for transfers between devices  148 us (14%)
  blocking collectives  140 us (13%)
  local copies, waits for them, and re-layouts  96.5 us (9%)
  other arithmetic  76.1 us (7%)
  between operations  18.3 us (2%)
    pallas_call x18, Pallas kernels, sum_rows(): pl.pallas_call(lambda *refs: sum_kernel(count, backward, gather, *refs),...  179 us
    pallas_call x6, Pallas kernels, send_results(): pl.pallas_call(lambda *refs: exchange_kernel(dp_count, *refs), out_shape=...  134 us
    pallas_call x6, Pallas kernels, send_rows(): pl.pallas_call(lambda *refs: dispatch_kernel(dp_count, tensor_count, *ref...  107 us
    all_gather x3, blocking collectives, on_device(): lax.all_gather(projected[:, head_width:], 'dp', axis=0, tiled=True)  77 us
    unnamed x10, waiting for transfers between devices  73 us
    reduce_scatter x1, waiting for transfers between devices, on_device(): lax.psum_scatter(jnp.concatenate([grad_sums[2], grad_sums[3]], axis=1).as...  64.5 us
    all_gather x6, blocking collectives, rows_in(): return lax.all_gather(part, 'tensor', axis=0, tiled=True)  39.1 us
    unnamed x535, local copies, waits for them, and re-layouts  25.2 us
  transfers between devices with their start and end apart: 12, of which 7 were waited for; matrix products, arithmetic and copies ran while one was open for 18% of the time, Pallas kernels for 8%

profile of v1, /device:TPU:0, one launch (start us, length us, event | category | flops | bytes accessed | tf_op | source)
XLA Modules:
  0.0 1065.0 jit_solution(16911579394507878197)
XLA Ops:
  12.1 23.4 %all-gather = bf16[16384]{0:T(1024)(128)(2,1)S(1)} all-gather(bf16[1024]{0:T(1024)(128)(2,1)S(1)} %fusion.393), channel_id=2, replica_groups=mesh['section'=2,'dp'=4,'tensor'=4] {'dp','tensor'}, dimensions={0}, use_global_device_ids=true | all-gather | bytes 34816 | tf_op jit(solution)/shard_map/all_gather | solution.py:341
  41.9 19.5 %copy.303 = pred[32,256,384]{2,0,1:T(32,128)(4,1)} copy(pred[32,256,384]{1,0,2:T(32,128)(4,1)S(1)} %iota_compare_fusion) | data formatting | bytes 6291456 | tf_op jit(solution)/shard_map/eq | solution.py:379
  96.2 30.2 %all_gather.43 = bf16[1024,384]{0,1:T(8,128)(2,1)S(1)} all-gather(bf16[256,384]{0,1:T(8,128)(2,1)S(1)} %slice.402), channel_id=1, replica_groups=mesh['section'=2,'dp'=4,'tensor'=4] {'dp'}, dimensions={0}, use_global_device_ids=true | all-gather | bytes 983040 | tf_op jit(solution)/shard_map/all_gather | solution.py:476
  148.3 12.6 %shard_map.204 = (f32[64,768]{1,0:T(8,128)S(1)}, bf16[4,64,768]{2,1,0:T(8,128)(2,1)S(1)}) custom-call(f32[4,64,768]{2,1,0:T(8,128)S(1)} %bitcast.664, f32[64,768]{1,0:T(8,128)S(1)} %get-tuple-element.84.refs_1_, f32[1,768]{1,0:T(1,128)S(1)} %slice.343.refs_2_.refs_3_), custom_call_target="tpu_custom_call" | custom-call | tf_op jit(solution)/shard_map/pallas_call | solution.py:183
  161.4 15.5 %shard_map.205 = bf16[4,160,768]{2,1,0:T(8,128)(2,1)S(1)} custom-call(bf16[4,160,768]{2,1,0:T(8,128)(2,1)S(1)} %bitcast.652), custom_call_target="tpu_custom_call" | custom-call | tf_op jit(solution)/shard_map/pallas_call | solution.py:243
  179.2 20.4 %shard_map.206 = bf16[4,160,768]{2,1,0:T(8,128)(2,1)S(1)} custom-call(bf16[4,160,768]{2,1,0:T(8,128)(2,1)S(1)} %bitcast.653), custom_call_target="tpu_custom_call" | custom-call | tf_op jit(solution)/shard_map/pallas_call | solution.py:279
  226.7 23.1 %all_gather.46 = bf16[1024,384]{0,1:T(8,128)(2,1)S(1)} all-gather(bf16[256,384]{0,1:T(8,128)(2,1)S(1)} %slice.418), channel_id=1, replica_groups=mesh['section'=2,'dp'=4,'tensor'=4] {'dp'}, dimensions={0}, use_global_device_ids=true | all-gather | bytes 983040 | tf_op jit(solution)/shard_map/all_gather | solution.py:476
  289.4 16.3 %shard_map.210 = bf16[4,160,768]{2,1,0:T(8,128)(2,1)S(1)} custom-call(bf16[4,160,768]{2,1,0:T(8,128)(2,1)S(1)} %bitcast.654), custom_call_target="tpu_custom_call" | custom-call | tf_op jit(solution)/shard_map/pallas_call | solution.py:243
  308.1 20.4 %shard_map.211 = bf16[4,160,768]{2,1,0:T(8,128)(2,1)S(1)} custom-call(bf16[4,160,768]{2,1,0:T(8,128)(2,1)S(1)} %bitcast.655), custom_call_target="tpu_custom_call" | custom-call | tf_op jit(solution)/shard_map/pallas_call | solution.py:279
  348.1 20.3 %shard_map.218 = bf16[4,160,768]{2,1,0:T(8,128)(2,1)S(1)} custom-call(bf16[4,160,768]{2,1,0:T(8,128)(2,1)S(1)} %bitcast.686), custom_call_target="tpu_custom_call" | custom-call | tf_op jit(solution)/shard_map/pallas_call | solution.py:243
  371.5 20.6 %shard_map.219 = bf16[4,160,768]{2,1,0:T(8,128)(2,1)S(1)} custom-call(bf16[4,160,768]{2,1,0:T(8,128)(2,1)S(1)} %bitcast.656), custom_call_target="tpu_custom_call" | custom-call | tf_op jit(solution)/shard_map/pallas_call | solution.py:279
  403.8 23.7 %all_gather.48 = bf16[1024,384]{0,1:T(8,128)(2,1)S(1)} all-gather(bf16[256,384]{0,1:T(8,128)(2,1)S(1)} %slice.426), channel_id=1, replica_groups=mesh['section'=2,'dp'=4,'tensor'=4] {'dp'}, dimensions={0}, use_global_device_ids=true | all-gather | bytes 983040 | tf_op jit(solution)/shard_map/all_gather | solution.py:476
  467.5 12.3 %shard_map.220 = (f32[64,768]{1,0:T(8,128)S(1)}, f32[1,768]{1,0:T(1,128)S(1)}, bf16[4,64,768]{2,1,0:T(8,128)(2,1)S(1)}) custom-call(f32[4,64,768]{2,1,0:T(8,128)S(1)} %bitcast.661, f32[64,768]{1,0:T(8,128)S(1)} %copy-done.49, f32[64,768]{1,0:T(8,128)S(1)} %get-tuple-element.273.refs_2_, f32[1,768]{1,0:T(1,128)S(1)} %slice.343.refs_2_.refs_3_), custom_call_target="tpu_custom_call" | custom-call | tf_op jit(solution)/shard_map/pallas_call | solution.py:183
  503.0 16.1 %shard_map.215 = bf16[4,160,768]{2,1,0:T(8,128)(2,1)S(1)} custom-call(bf16[4,160,768]{2,1,0:T(8,128)(2,1)S(1)} %bitcast.657), custom_call_target="tpu_custom_call" | custom-call | tf_op jit(solution)/shard_map/pallas_call | solution.py:243
  526.0 31.9 %shard_map.216 = bf16[4,160,768]{2,1,0:T(8,128)(2,1)S(1)} custom-call(bf16[4,160,768]{2,1,0:T(8,128)(2,1)S(1)} %bitcast.658), custom_call_target="tpu_custom_call" | custom-call | tf_op jit(solution)/shard_map/pallas_call | solution.py:279
  613.1 20.3 %shard_map.223 = bf16[4,160,768]{2,1,0:T(8,128)(2,1)S(1)} custom-call(bf16[4,160,768]{2,1,0:T(8,128)(2,1)S(1)} %bitcast.687), custom_call_target="tpu_custom_call" | custom-call | tf_op jit(solution)/shard_map/pallas_call | solution.py:243
  636.5 20.3 %shard_map.224 = bf16[4,160,768]{2,1,0:T(8,128)(2,1)S(1)} custom-call(bf16[4,160,768]{2,1,0:T(8,128)(2,1)S(1)} %bitcast.659), custom_call_target="tpu_custom_call" | custom-call | tf_op jit(solution)/shard_map/pallas_call | solution.py:279
  671.5 12.1 %shard_map.226 = (f32[64,768]{1,0:T(8,128)S(1)}, f32[1,768]{1,0:T(1,128)S(1)}, bf16[4,64,768]{2,1,0:T(8,128)(2,1)S(1)}) custom-call(f32[4,64,768]{2,1,0:T(8,128)S(1)} %bitcast.694, f32[64,768]{1,0:T(8,128)S(1)} %get-tuple-element.101.refs_1_, f32[64,768]{1,0:T(8,128)S(1)} %copy-done.46, f32[1,768]{1,0:T(1,128)S(1)} %slice.335.refs_2_.refs_3_), custom_call_target="tpu_custom_call" | custom-call | tf_op jit(solution)/shard_map/pallas_call | solution.py:183
  747.7 18.4 %shard_map.228 = bf16[4,160,768]{2,1,0:T(8,128)(2,1)S(1)} custom-call(bf16[4,160,768]{2,1,0:T(8,128)(2,1)S(1)} %bitcast.688), custom_call_target="tpu_custom_call" | custom-call | tf_op jit(solution)/shard_map/pallas_call | solution.py:243
  769.3 20.3 %shard_map.229 = bf16[4,160,768]{2,1,0:T(8,128)(2,1)S(1)} custom-call(bf16[4,160,768]{2,1,0:T(8,128)(2,1)S(1)} %bitcast.660), custom_call_target="tpu_custom_call" | custom-call | tf_op jit(solution)/shard_map/pallas_call | solution.py:279
  804.3 12.1 %shard_map.231 = (f32[64,768]{1,0:T(8,128)S(1)}, f32[1,768]{1,0:T(1,128)S(1)}, bf16[4,64,768]{2,1,0:T(8,128)(2,1)S(1)}) custom-call(f32[4,64,768]{2,1,0:T(8,128)S(1)} %bitcast.689, f32[64,768]{1,0:T(8,128)S(1)} %get-tuple-element.106.refs_1_, f32[64,768]{1,0:T(8,128)S(1)} %copy-done.44, f32[1,768]{1,0:T(1,128)S(1)} %slice.335.refs_2_.refs_3_), custom_call_target="tpu_custom_call" | custom-call | tf_op jit(solution)/shard_map/pallas_call | solution.py:183
  907.8 46.0 %all-reduce.5.cloned.1.call-done = f32[16,1024]{1,0:T(8,128)} async-done(((f32[16,1024]{1,0:T(8,128)}), f32[16,1024]{1,0:T(8,128)}) %all-reduce.5.cloned.1.call-update) | async-done | bytes 65552
  960.2 26.8 %reduce-scatter.16.cloned.1.call-done = bf16[192,768]{1,0:T(8,128)(2,1)} async-done(((bf16[768,768]{1,0:T(8,128)(2,1)}), bf16[192,768]{1,0:T(8,128)(2,1)}) %reduce-scatter.16.cloned.1.call-update) | async-done | bytes 294928
  990.1 64.5 %reduce-scatter.14.cloned.1.call-done = bf16[192,2304]{1,0:T(8,128)(2,1)} async-done(((bf16[768,2304]{1,0:T(8,128)(2,1)}), bf16[192,2304]{1,0:T(8,128)(2,1)}) %reduce-scatter.14.cloned.1.call-update) | async-done | bytes 884752 | tf_op jit(solution)/shard_map/reduce_scatter | solution.py:749
  (907 shorter events, 499.4 us)
Async XLA Ops:
  7.2 170.6 %copy-start = (bf16[1,2,768,768]{3,2,1,0:T(8,128)(2,1)S(1)}, bf16[1,2,768,768]{3,2,1,0:T(8,128)(2,1)}, u32[]{:S(2)}) copy-start(bf16[1,2,768,768]{3,2,1,0:T(8,128)(2,1)} %param.28) | copy-start | bytes 7077892
  7.2 87.3 %all-gather.5.cloned.1.call-start = ((), (), s32[]{:S(2)}) async-start(), calls=%async_computation.5 | async-start | bytes 1474560 | tf_op jit(solution)/shard_map/all_gather | solution.py:320
  10.3 132.7 %all-gather.7.cloned.1.call-start = ((), (), s32[]{:S(2)}) async-start(), calls=%async_computation.6 | async-start | bytes 4423680 | tf_op jit(solution)/shard_map/all_gather | solution.py:326
  11.5 577.8 %reduce-scatter.8.cloned.1.call-start = ((), (), s32[]{:S(2)}) async-start(), calls=%async_computation.7 | async-start | bytes 983040 | tf_op jit(solution)/shard_map/reduce_scatter | solution.py:704
  69.9 149.2 %copy-start.218 = (f32[768]{0:T(1024)}, f32[768]{0:T(1024)S(1)}, u32[]{:S(2)}) copy-start(f32[768]{0:T(1024)S(1)} %mul.608) | copy-start | bytes 9220
  88.1 39.2 %copy-start.93 = (pred[256,1024]{1,0:T(8,128)(4,1)}, pred[256,1024]{1,0:T(8,128)(4,1)S(1)}, u32[]{:S(2)}) copy-start(pred[256,1024]{1,0:T(8,128)(4,1)S(1)} %compare_and_fusion) | copy-start | bytes 786436
  96.2 31.1 %copy-start.147 = (bf16[256,192]{0,1:T(8,128)(2,1)}, bf16[256,192]{0,1:T(8,128)(2,1)S(1)}, u32[]{:S(2)}) copy-start(bf16[256,192]{0,1:T(8,128)(2,1)S(1)} %slice.404) | copy-start | bytes 294916
  160.9 41.7 %copy-start.8 = (bf16[4,64,768]{2,1,0:T(8,128)(2,1)}, bf16[4,64,768]{2,1,0:T(8,128)(2,1)S(1)}, u32[]{:S(2)}) copy-start(bf16[4,64,768]{2,1,0:T(8,128)(2,1)S(1)} %get-tuple-element.85) | copy-start | bytes 1179652
  212.0 6.3 collective-permute-start
  219.0 30.8 %copy-start.158 = (bf16[64,768]{1,0:T(8,128)(2,1)}, bf16[64,768]{1,0:T(8,128)(2,1)S(1)}, u32[]{:S(2)}) copy-start(bf16[64,768]{1,0:T(8,128)(2,1)S(1)} %get-tuple-element.205) | copy-start | bytes 294916
  225.5 26.1 %copy-start.153 = (bf16[256,768]{1,0:T(8,128)(2,1)}, bf16[256,768]{1,0:T(8,128)(2,1)S(1)}, u32[]{:S(2)}) copy-start(bf16[256,768]{1,0:T(8,128)(2,1)S(1)} %all_gather.45) | copy-start | bytes 1179652
  289.0 42.6 %copy-start.6 = (bf16[4,64,768]{2,1,0:T(8,128)(2,1)}, bf16[4,64,768]{2,1,0:T(8,128)(2,1)S(1)}, u32[]{:S(2)}) copy-start(bf16[4,64,768]{2,1,0:T(8,128)(2,1)S(1)} %get-tuple-element.89) | copy-start | bytes 1179652
  343.1 27.1 %copy-start.200 = (bf16[64,768]{1,0:T(8,128)(2,1)}, bf16[64,768]{1,0:T(8,128)(2,1)S(1)}, u32[]{:S(2)}) copy-start(bf16[64,768]{1,0:T(8,128)(2,1)S(1)} %get-tuple-element.198) | copy-start | bytes 294916
  343.1 52.0 %collective-permute-start.1 = (bf16[64,768]{1,0:T(8,128)(2,1)S(1)}, bf16[64,768]{1,0:T(8,128)(2,1)S(1)}, u32[]{:S(2)}, u32[]{:S(2)}) collective-permute-start(bf16[64,768]{1,0:T(8,128)(2,1)S(1)} %get-tuple-element.198), channel_id=1, source_target_pairs={{0,16},{1,17},{2,18},{3,19},{4,20},{5,21},{6,22},{7,23},{8,24},{9,... | collective-permute-start | bytes 294920 | tf_op jit(solution)/shard_map/ppermute | solution.py:22
  466.5 36.1 %copy-start.10 = (bf16[4,64,768]{2,1,0:T(8,128)(2,1)}, bf16[4,64,768]{2,1,0:T(8,128)(2,1)S(1)}, u32[]{:S(2)}) copy-start(bf16[4,64,768]{2,1,0:T(8,128)(2,1)S(1)} %get-tuple-element.93) | copy-start | bytes 1179652
  523.3 196.2 %reduce-scatter.10.cloned.1.call-start = ((), (), s32[]{:S(2)}) async-start(), calls=%async_computation.8 | async-start | bytes 983040 | tf_op jit(solution)/shard_map/reduce_scatter | solution.py:704
  597.2 7.2 collective-permute-start.2
  636.5 32.9 %copy-start.168 = (f32[256,1536]{1,0:T(8,128)S(1)}, f32[256,1536]{1,0:T(8,128)}, u32[]{:S(2)}) copy-start(f32[256,1536]{1,0:T(8,128)} %get-tuple-element.226) | copy-start | bytes 4718596
  692.6 159.7 %reduce-scatter.12.cloned.1.call-start = ((), (), s32[]{:S(2)}) async-start(), calls=%async_computation.9 | async-start | bytes 983040 | tf_op jit(solution)/shard_map/reduce_scatter | solution.py:704
  728.6 7.7 collective-permute-start.3
  769.3 32.9 %copy-start.167 = (f32[256,1536]{1,0:T(8,128)S(1)}, f32[256,1536]{1,0:T(8,128)}, u32[]{:S(2)}) copy-start(f32[256,1536]{1,0:T(8,128)} %get-tuple-element.225) | copy-start | bytes 4718596
  825.1 128.7 %all-reduce.5.cloned.1.call-start = ((), (), s32[]{:S(2)}) async-start(), calls=%async_computation.12 | async-start | bytes 131072
  865.6 121.5 %reduce-scatter.16.cloned.1.call-start = ((), (), s32[]{:S(2)}) async-start(), calls=%async_computation.11 | async-start | bytes 1474560
  871.9 182.7 %reduce-scatter.14.cloned.1.call-start = ((), (), s32[]{:S(2)}) async-start(), calls=%async_computation.10 | async-start | bytes 4423680 | tf_op jit(solution)/shard_map/reduce_scatter | solution.py:749
  (251 other events, 1756.5 us)
Sparse Core Ops, SparseCore 0:
  10.4 32.7 all-gather.4
  44.8 82.0 all-gather.6
  523.4 35.7 reduce-scatter.7
  692.7 26.6 reduce-scatter.9
  825.3 26.8 reduce-scatter.11
  865.7 88.1 all-reduce.4
  956.3 30.7 reduce-scatter.15
  989.5 65.0 reduce-scatter.13
